TPU v7x, 256 devices: a whole 4x4x8 slice. The times are simulated.
256 devices in a mesh: dp: 16 (over z, core), tensor: 16 (over y, x).
Axes of the slice: x: 4, y: 4, z: 8, core: 2. Of those that a mesh axis runs over, the one named last changes fastest.
Arguments:
- grads: bfloat16 [16, 8192, 2048], P('dp', None, 'tensor'), may hold values from -200 to 200, as said below
- error: float32 [16, 8192, 2048], P('dp', None, 'tensor'), may hold values from -4 to 4
- q_prev: float32 [2048, 32], P('tensor'), may hold values from -5 to 5
Outputs:
- synced: bfloat16 [8192, 2048], P('dp', 'tensor')
- error_out: float32 [16, 8192, 2048], P('dp', None, 'tensor')
- q_new: float32 [2048, 32], P('tensor')
Inputs may be any that keep to these rules, and one draw needn't show every extreme that they name: `grads`: each replica's gradient is finite.
All inputs are finite; a program needn't handle non-finite values.
Results may differ from a plain program's by a relative error of at most 0.001.
Values sent between devices are 32-bit elements; how exact they have to be, the bound alone decides.
A program may use at most 64 MiB of HBM per device.

v0:
```python
import jax
import jax.numpy as jnp
from jax import lax
from jax.sharding import PartitionSpec as P


def on_device(grads, error, q_prev):
    highest = lax.Precision.HIGHEST
    merged = grads.astype(jnp.float32) + error
    local = merged[0]
    partial_p = jnp.dot(local, q_prev, precision=highest)
    p_whole = lax.psum(partial_p, ("dp", "tensor"))
    gram = jnp.dot(p_whole.T, p_whole, precision=highest)
    lower = jnp.linalg.cholesky(gram)
    basis = lax.linalg.triangular_solve(
        lower, p_whole, left_side=False, lower=True, transpose_a=True
    )
    replicas = lax.axis_size("dp")
    q_terms = jnp.dot(local.T, basis, precision=highest)
    q_new = lax.psum(q_terms, "dp") / replicas
    approx = jnp.dot(basis, q_new.T, precision=highest)
    error_out = merged - approx[None]
    own_rows = approx.shape[0] // replicas
    first_row = lax.axis_index("dp") * own_rows
    synced = lax.dynamic_slice_in_dim(approx, first_row, own_rows, 0).astype(jnp.bfloat16)
    return (synced, error_out, q_new)


def solution(mesh):
    placed = (P("dp", None, "tensor"), P("dp", None, "tensor"), P("tensor", None))
    return jax.shard_map(
        on_device,
        mesh=mesh,
        in_specs=placed,
        out_specs=(P("dp", "tensor"), P("dp", None, "tensor"), P("tensor", None)),
        check_vma=False,
    )
```

profile of v0, /device:TPU:1, one launch (start us, length us, event | category | flops | bytes accessed | tf_op | source)
XLA Modules:
  0.0 353.8 jit_solution(3670249582008717158)
XLA Ops:
  7.2 0.0 copy-start
  7.2 0.0 all-reduce.2.cloned.1.call-start
  7.2 0.7 copy-done
  7.9 8.1 %fusion.2 = f32[8192,32]{0,1:T(8,128)} fusion(f32[128,32]{0,1:T(8,128)S(1)} %copy-done, f32[1,8192,128]{2,1,0:T(8,128)} %param.4, bf16[1,8192,128]{2,1,0:T(8,128)(2,1)} %param.3), kind=kOutput, calls=%fused_computation.3 | convolution fusion | flops 404750336 | bytes 7356416 | tf_op jit(solution)/shard_map/dot_general | solution.py:11
  16.0 0.0 copy-start.1
  16.0 0.0 all-reduce.2.cloned.1.call-update
  16.0 258.4 %all-reduce.2.cloned.1.call-done = f32[8192,32]{0,1:T(8,128)} async-done(((f32[8192,32]{0,1:T(8,128)}), f32[8192,32]{0,1:T(8,128)}) %all-reduce.2.cloned.1.call-update) | async-done | bytes 1048592 | tf_op jit(solution)/shard_map/psum | solution.py:12
  274.4 2.5 fusion.8
  276.9 0.1 copy.6
  277.0 2.9 cholesky.16
  280.0 0.6 compare_reduce_fusion
  280.6 0.7 fusion.4
  281.3 2.4 custom-call.6
  283.7 2.3 fusion.5
  286.0 0.0 copy-done.1
  286.0 4.9 %fusion = f32[128,32]{0,1:T(8,128)S(1)} fusion(f32[8192,32]{0,1:T(8,128)S(1)} %fusion.5, f32[1,8192,128]{2,1,0:T(8,128)} %param.4, bf16[1,8192,128]{2,1,0:T(8,128)(2,1)S(1)} %copy-done.1), kind=kOutput, calls=%fused_computation.1 | convolution fusion | flops 404750336 | bytes 7356416 | tf_op jit(solution)/shard_map/dot_general | solution.py:19
  290.9 45.6 %psum.15 = f32[128,32]{0,1:T(8,128)S(1)} all-reduce(f32[128,32]{0,1:T(8,128)S(1)} %fusion), channel_id=1, replica_groups=mesh['dp'=16,'tensor'=16] {'dp'}, use_global_device_ids=true, to_apply=%region_3.4 | all-reduce | flops 4096 | bytes 32768 | tf_op jit(solution)/shard_map/psum | solution.py:20
  336.5 0.0 copy-start.2
  336.5 9.8 %bitcast_subtract_fusion = (f32[1,8192,128]{2,1,0:T(8,128)}, bf16[8192,128]{1,0:T(8,128)(2,1)S(1)}) fusion(f32[1,8192,128]{2,1,0:T(8,128)} %param.4, bf16[1,8192,128]{2,1,0:T(8,128)(2,1)S(1)} %copy-done.1, f32[8192,32]{0,1:T(8,128)S(1)} %fusion.5, f32[128,32]{0,1:T(8,128)S(1)} %broadcast_multiply_fusion), kind=kOutput, calls=%fused_computation | convolution fusion | flops 406847488 | bytes 13647872 | tf_op jit(solution)/shard_map/dot_general | solution.py:21
  346.3 0.0 copy-done.2
  346.3 0.7 dynamic-slice_convert_fusion
  (3 shorter events, 0.0 us)
Async XLA Ops:
  7.2 0.7 copy-start
  7.2 267.2 %all-reduce.2.cloned.1.call-start = ((), (), s32[]{:S(2)}) async-start(), calls=%async_computation | async-start | bytes 2097152 | tf_op jit(solution)/shard_map/psum | solution.py:12
  16.0 270.0 %copy-start.1 = (bf16[1,8192,128]{2,1,0:T(8,128)(2,1)S(1)}, bf16[1,8192,128]{2,1,0:T(8,128)(2,1)}, u32[]{:S(2)}) copy-start(bf16[1,8192,128]{2,1,0:T(8,128)(2,1)} %param.3) | copy-start | bytes 6291460
  336.5 9.8 %copy-start.2 = (f32[128,32]{0,1:T(8,128)}, f32[128,32]{0,1:T(8,128)S(1)}, u32[]{:S(2)}) copy-start(f32[128,32]{0,1:T(8,128)S(1)} %broadcast_multiply_fusion) | copy-start | bytes 49156
Sparse Core Ops, SparseCore 0:
  16.1 258.2 all-reduce.1
where the time goes:
time: 356 us; the launch traced here: 354 us
  waiting for transfers between devices  258 us (72%)
  blocking collectives  45.6 us (13%)
  matrix products  27.6 us (8%)
  between operations  14.1 us (4%)
  other arithmetic  6.69 us (2%)
    psum x1, waiting for transfers between devices, on_device(): p_whole = lax.psum(partial_p, ('dp', 'tensor'))  258 us
    psum x1, blocking collectives, on_device(): q_new = lax.psum(q_terms, 'dp') / replicas  45.6 us
    dot_general x1, matrix products, on_device(): approx = jnp.dot(basis, q_new.T, precision=highest)  9.81 us
    dot_general x1, matrix products, on_device(): partial_p = jnp.dot(local, q_prev, precision=highest)  8.09 us
  transfers between devices with their start and end apart: 1, of which 1 were waited for; matrix products, arithmetic and copies ran while one was open for 0% of the time, Pallas kernels for 0%

commit v1 on v0

v1 whole, which is shorter than its diff:
```python
import jax
import jax.numpy as jnp
from jax import lax
from jax.experimental import pallas as pl
from jax.experimental.pallas import tpu as pltpu
from jax.sharding import PartitionSpec as P

MESH = pl.DeviceIdType.MESH
F32, BF16 = jnp.float32, jnp.bfloat16
D, COLS, RANK = 8192, 128, 32
X, Y, Z = 4, 4, 8
LANES = 128
BLOCKS = D // LANES
HALF = BLOCKS // 2
PIECE = HALF // (X * Y)
CHUNK = 1024
NCHUNK = D // CHUNK
PER = CHUNK // LANES
OFFSETS = sorted(
    [(i, j) for j in range(Y) for i in range(X) if (i, j) != (0, 0)],
    key=lambda o: -(min(o[0], X - o[0]) + min(o[1], Y - o[1])),
)
NT = (((1,), (1,)), ((), ()))
TN = (((0,), (0,)), ((), ()))


def dot(a, b, dims=(((1,), (0,)), ((), ())), precision=None):
    return lax.dot_general(a, b, dims, precision=precision, preferred_element_type=F32)


def pair(value):
    hi = value.astype(BF16)
    return hi, (value - hi.astype(F32)).astype(BF16)


def quarters(value, rows, columns):
    return (
        value[:rows, :columns]
        + value[:rows, columns:]
        + value[rows:, :columns]
        + value[rows:, columns:]
    )


def inverse_factor(gram):
    n = gram.shape[0]
    row = lax.broadcasted_iota(jnp.int32, (n, n), 0)
    col = lax.broadcasted_iota(jnp.int32, (n, n), 1)
    left, right = gram, jnp.where(row == col, 1.0, 0.0).astype(F32)
    for k in range(n):
        scale = left[:, k : k + 1] / left[k : k + 1, k : k + 1]
        scale = jnp.where(row[:, :1] > k, scale, 0.0)
        left, right = (
            left - scale * left[k : k + 1, :],
            right - scale * right[k : k + 1, :],
        )
    pivots = jnp.sum(jnp.where(row == col, left, 0.0), axis=1, keepdims=True)
    return right / jnp.sqrt(pivots)


def share_kernel(
    q_ref, g_hbm, e_hbm, merged, p_rows, linv_ref, terms_ref,
    g_in, e_in, pairs, part, sib, summed, from_xy, from_z, p_all, p_pairs, from_zt, t_mine, t_sib,
    ld_g, ld_e, sib_s, sib_r, xy_s, xy_r, z_s, z_r, ag_s, ag_r, fw_s, fw_r, tz_s, tz_r, tc_s, tc_r,
):
    dp, me = lax.axis_index("dp"), lax.axis_index("tensor")
    x, y = lax.rem(me, X), lax.div(me, X)
    z, core = lax.div(dp, 2), lax.rem(dp, 2)
    other = 1 - core

    def at_xy(dx, dy):
        return lax.rem(y + dy, Y) * X + lax.rem(x + dx, X)

    def at_z(dz):
        return lax.rem(z + dz, Z)

    sibling = (z * 2 + other, me)

    loads = []
    for i in range(NCHUNK):
        where = (other if i < NCHUNK // 2 else core) * (NCHUNK // 2) + i % (NCHUNK // 2)
        rows = pl.ds(pl.multiple_of(where * CHUNK, CHUNK), CHUNK)
        pair_of = (
            pltpu.make_async_copy(g_hbm.at[0, rows], g_in.at[rows], ld_g.at[i]),
            pltpu.make_async_copy(e_hbm.at[0, rows], e_in.at[rows], ld_e.at[i]),
        )
        for c in pair_of:
            c.start()
        loads.append((where, pair_of))

    barrier = pltpu.get_barrier_semaphore()
    pl.semaphore_signal(barrier, inc=1, device_id=sibling, device_id_type=MESH)
    for dx, dy in OFFSETS:
        pl.semaphore_signal(barrier, inc=1, device_id=(dp, at_xy(dx, dy)), device_id_type=MESH)
    for k in range(1, Z):
        pl.semaphore_signal(barrier, inc=1, device_id=(at_z(k) * 2 + core, me), device_id_type=MESH)

    qh, ql = pair(q_ref[...])
    q_pairs = jnp.concatenate(
        [jnp.concatenate([qh, qh], axis=1), jnp.concatenate([ql, ql], axis=1)], axis=0
    )

    def partial(i):
        where, pair_of = loads[i]
        for c in pair_of:
            c.wait()
        base = where * CHUNK

        def tile(j, _):
            rows = pl.ds(pl.multiple_of(base + j * 256, 256), 256)
            total = g_in[rows].astype(F32) + e_in[rows]
            merged[rows] = total
            hi, lo = pair(total)
            both = jnp.concatenate([hi, lo], axis=1)
            pairs[rows] = both
            out = dot(q_pairs, both, NT)
            out = out[:RANK] + out[RANK:]
            first = where * PER + j * 2
            part[first] = out[:, :LANES]
            part[first + 1] = out[:, LANES:]
            return 0

        lax.fori_loop(0, CHUNK // 256, tile, 0, unroll=True)

    for i in range(NCHUNK // 2):
        partial(i)
    pl.semaphore_wait(barrier, 1 + len(OFFSETS) + Z - 1)

    def to_sibling(i):
        return pltpu.make_async_remote_copy(
            src_ref=part.at[pl.ds(other * HALF + i * PER, PER)], dst_ref=sib.at[pl.ds(i * PER, PER)],
            send_sem=sib_s.at[i], recv_sem=sib_r.at[i], device_id=sibling, device_id_type=MESH,
        )

    for i in range(NCHUNK // 2):
        to_sibling(i).start()
    for i in range(NCHUNK // 2, NCHUNK):
        partial(i)
    for i in range(NCHUNK // 2):
        to_sibling(i).wait()

    def scatter(j):
        to = at_xy(*OFFSETS[j])
        return to, pltpu.make_async_remote_copy(
            src_ref=summed.at[pl.ds(to * PIECE, PIECE)], dst_ref=from_xy.at[j],
            send_sem=xy_s.at[j], recv_sem=xy_r.at[j], device_id=(dp, to), device_id_type=MESH,
        )

    for j in range(len(OFFSETS)):
        to, copy = scatter(j)
        piece = pl.ds(to * PIECE, PIECE)
        summed[piece] = part[pl.ds(core * HALF + to * PIECE, PIECE)] + sib[piece]
        copy.start()
    own = pl.ds(me * PIECE, PIECE)
    mine = pl.ds(core * HALF + me * PIECE, PIECE)
    total = part[mine] + sib[own]
    for j in reversed(range(len(OFFSETS))):
        scatter(j)[1].wait()
        total = total + from_xy[j]
    from_z[z] = total

    def along_z(k, buffer, s, r):
        to = at_z(k)
        return to, pltpu.make_async_remote_copy(
            src_ref=buffer.at[z], dst_ref=buffer.at[z],
            send_sem=s.at[k], recv_sem=r.at[z], device_id=(to * 2 + core, me), device_id_type=MESH,
        )

    def z_arrived(k, buffer, s, r):
        origin = at_z(k)
        pltpu.make_async_remote_copy(
            src_ref=buffer.at[origin], dst_ref=buffer.at[origin],
            send_sem=s.at[k], recv_sem=r.at[origin], device_id=(origin * 2 + core, me), device_id_type=MESH,
        ).wait_recv()

    z_order = (4, 3, 5, 2, 6, 1, 7)
    for k in z_order:
        along_z(k, from_z, z_s, z_r)[1].start()
    for k in reversed(z_order):
        z_arrived(k, from_z, z_s, z_r)
    total = from_z[0]
    for k in range(1, Z):
        total = total + from_z[k]
    p_all[mine] = total

    def gather(j):
        return pltpu.make_async_remote_copy(
            src_ref=p_all.at[mine], dst_ref=p_all.at[mine],
            send_sem=ag_s.at[j], recv_sem=ag_r.at[j], device_id=(dp, at_xy(*OFFSETS[j])), device_id_type=MESH,
        )

    def forward(j, half):
        dx, dy = OFFSETS[j] if j < len(OFFSETS) else (0, 0)
        piece = pl.ds(half * HALF + at_xy(X - dx, Y - dy) * PIECE, PIECE)
        return pltpu.make_async_remote_copy(
            src_ref=p_all.at[piece], dst_ref=p_all.at[piece],
            send_sem=fw_s.at[j], recv_sem=fw_r.at[j], device_id=sibling, device_id_type=MESH,
        )

    def gathered(j):
        dx, dy = OFFSETS[j]
        piece = pl.ds(core * HALF + at_xy(X - dx, Y - dy) * PIECE, PIECE)
        pltpu.make_async_remote_copy(
            src_ref=p_all.at[piece], dst_ref=p_all.at[piece],
            send_sem=ag_s.at[j], recv_sem=ag_r.at[j], device_id=(dp, at_xy(dx, dy)), device_id_type=MESH,
        ).wait_recv()

    for j in range(len(OFFSETS)):
        gather(j).start()
    forward(len(OFFSETS), core).start()
    for j in reversed(range(len(OFFSETS))):
        gathered(j)
        forward(j, core).start()

    def terms(half, acc):
        def step(i, acc):
            chunk = half * (NCHUNK // 2) + i
            blocks = p_all[pl.ds(chunk * PER, PER)]
            hi, lo = pair(jnp.concatenate([blocks[b] for b in range(PER)], axis=1))
            both = jnp.concatenate([hi, lo], axis=0)
            p_pairs[chunk] = both
            rows = pl.ds(pl.multiple_of(chunk * CHUNK, CHUNK), CHUNK)
            return acc + dot(both, pairs[rows])

        return lax.fori_loop(0, NCHUNK // 2, step, acc)

    acc = terms(core, jnp.zeros((2 * RANK, 2 * COLS), F32))
    for j in reversed(range(len(OFFSETS) + 1)):
        forward(j, other).wait_recv()
    acc = terms(other, acc)
    from_zt[z] = quarters(acc, RANK, COLS)
    for k in z_order:
        along_z(k, from_zt, tz_s, tz_r)[1].start()

    def gram_step(i, acc):
        both = p_pairs[i]
        return acc + dot(both, both, NT)

    gram = lax.fori_loop(0, NCHUNK, gram_step, jnp.zeros((2 * RANK, 2 * RANK), F32))
    linv_ref[...] = inverse_factor(quarters(gram, RANK, RANK))

    def turn(b, _):
        block = p_all[b]
        hi = block.astype(BF16).astype(F32)
        lo = block - hi
        stacked = jnp.concatenate([hi, lo, hi, lo], axis=0)
        p_rows[pl.ds(pl.multiple_of(b * LANES, LANES), LANES)] = stacked.T.astype(BF16)
        return 0

    lax.fori_loop(0, BLOCKS, turn, 0, unroll=4)

    for k in reversed(z_order):
        z_arrived(k, from_zt, tz_s, tz_r)
    total = from_zt[0]
    for k in range(1, Z):
        total = total + from_zt[k]
    t_mine[...] = total
    last = pltpu.make_async_remote_copy(
        src_ref=t_mine, dst_ref=t_sib, send_sem=tc_s, recv_sem=tc_r, device_id=sibling, device_id_type=MESH
    )
    last.start()
    for j in range(len(OFFSETS)):
        gather(j).wait_send()
    for j in range(len(OFFSETS) + 1):
        forward(j, core).wait_send()
    for k in z_order:
        along_z(k, from_z, z_s, z_r)[1].wait_send()
        along_z(k, from_zt, tz_s, tz_r)[1].wait_send()
    last.wait()
    terms_ref[...] = t_mine[...] + t_sib[...]


def share(q_t, grads, error):
    sems = pltpu.SemaphoreType.DMA
    n = len(OFFSETS)
    return pl.pallas_call(
        share_kernel,
        name="share",
        out_shape=(
            pltpu.VMEM((D, COLS), F32),
            pltpu.VMEM((D, LANES), BF16),
            pltpu.VMEM((RANK, RANK), F32),
            pltpu.VMEM((RANK, COLS), F32),
        ),
        in_specs=[
            pl.BlockSpec(memory_space=pltpu.VMEM),
            pl.BlockSpec(memory_space=pltpu.HBM),
            pl.BlockSpec(memory_space=pltpu.HBM),
        ],
        out_specs=[pl.BlockSpec(memory_space=pltpu.VMEM)] * 4,
        scratch_shapes=[
            pltpu.VMEM((D, COLS), BF16),
            pltpu.VMEM((D, COLS), F32),
            pltpu.VMEM((D, 2 * COLS), BF16),
            pltpu.VMEM((BLOCKS, RANK, LANES), F32),
            pltpu.VMEM((HALF, RANK, LANES), F32),
            pltpu.VMEM((HALF, RANK, LANES), F32),
            pltpu.VMEM((n, PIECE, RANK, LANES), F32),
            pltpu.VMEM((Z, PIECE, RANK, LANES), F32),
            pltpu.VMEM((BLOCKS, RANK, LANES), F32),
            pltpu.VMEM((NCHUNK, 2 * RANK, CHUNK), BF16),
            pltpu.VMEM((Z, RANK, COLS), F32),
            pltpu.VMEM((RANK, COLS), F32),
            pltpu.VMEM((RANK, COLS), F32),
            sems((NCHUNK,)), sems((NCHUNK,)),
            sems((NCHUNK // 2,)), sems((NCHUNK // 2,)),
            sems((n,)), sems((n,)),
            sems((Z,)), sems((Z,)),
            sems((n,)), sems((n,)),
            sems((n + 1,)), sems((n + 1,)),
            sems((Z,)), sems((Z,)),
            sems, sems,
        ],
        compiler_params=pltpu.CompilerParams(
            collective_id=0, has_side_effects=True, vmem_limit_bytes=32 * 1024 * 1024
        ),
    )(q_t, *(pltpu.with_memory_space_constraint(a, pltpu.HBM) for a in (grads, error)))


def finish_kernel(replicas, merged, p_rows, linv_ref, terms_ref, synced, error_out, q_ref, out, rows_out, sem, sem_rows):
    dp = lax.axis_index("dp")
    linv = linv_ref[...]
    highest = lax.Precision.HIGHEST
    q_t = dot(linv, terms_ref[...], precision=highest) / replicas
    q_ref[...] = q_t
    hi, lo = pair(dot(linv, q_t, TN, precision=highest))
    right = jnp.concatenate([hi, hi, lo, lo], axis=0)
    copies = []
    for i in range(NCHUNK):
        rows = pl.ds(i * CHUNK, CHUNK)
        out[rows] = merged[rows] - dot(p_rows[rows], right)
        copies.append(pltpu.make_async_copy(out.at[rows], error_out.at[0, rows], sem.at[i]))
        copies[-1].start()
    own = D // replicas
    rows_out[...] = dot(p_rows[pl.ds(pl.multiple_of(dp * own, own), own)], right).astype(BF16)
    copies.append(pltpu.make_async_copy(rows_out, synced, sem_rows))
    copies[-1].start()
    for c in copies:
        c.wait()


def finish(replicas, merged, p_rows, linv, terms):
    def body(*refs):
        finish_kernel(replicas, *refs)

    sems = pltpu.SemaphoreType.DMA
    own = D // replicas
    args = [pltpu.with_memory_space_constraint(a, pltpu.VMEM) for a in (merged, p_rows, linv, terms)]
    return pl.pallas_call(
        body,
        name="finish",
        out_shape=(
            jax.ShapeDtypeStruct((own, COLS), BF16),
            jax.ShapeDtypeStruct((1, D, COLS), F32),
            jax.ShapeDtypeStruct((RANK, COLS), F32),
        ),
        in_specs=[pl.BlockSpec(memory_space=pltpu.VMEM)] * 4,
        out_specs=[
            pl.BlockSpec(memory_space=pl.ANY),
            pl.BlockSpec(memory_space=pl.ANY),
            pl.BlockSpec(memory_space=pltpu.VMEM),
        ],
        scratch_shapes=[
            pltpu.VMEM((D, COLS), F32),
            pltpu.VMEM((own, COLS), BF16),
            sems((NCHUNK,)),
            sems,
        ],
        compiler_params=pltpu.CompilerParams(vmem_limit_bytes=16 * 1024 * 1024),
    )(*args)


def solution(mesh):
    replicas = mesh.shape["dp"]

    def on_device(grads, error, q_prev):
        merged, p_rows, linv, terms = share(q_prev.T, grads, error)
        synced, error_out, q_t = finish(replicas, merged, p_rows, linv, terms)
        return synced, error_out, q_t.T

    placed = (P("dp", None, "tensor"), P("dp", None, "tensor"), P("tensor", None))
    return jax.shard_map(
        on_device,
        mesh=mesh,
        in_specs=placed,
        out_specs=(P("dp", "tensor"), P("dp", None, "tensor"), P("tensor", None)),
        check_vma=False,
    )
```

time: 356 us -> 51.7 us (0.15)
  waiting for transfers between devices: 258 us -> 0 us
  Pallas kernels: 0 us -> 50.2 us
  blocking collectives: 45.6 us -> 0 us
  matrix products: 27.6 us -> 0 us
  between operations: 14.1 us -> 0.65 us
  other arithmetic: 6.69 us -> 0 us
    psum x1 -> x0, waiting for transfers between devices: 258 us -> none  [on_device(): p_whole = lax.psum(partial_p, ('dp', 'tensor'))]
    pallas_call x0 -> x2, Pallas kernels: none -> 50.2 us  [the longest x1 46.9 us: share(): pl.pallas_call(share_kernel, name='share', out_shape=(pltpu.VMEM((D, COLS...]
    psum x1 -> x0, blocking collectives: 45.6 us -> none  [on_device(): q_new = lax.psum(q_terms, 'dp') / replicas]
    dot_general x4 -> x0, matrix products: 25.3 us -> none  [the longest x1 9.81 us: on_device(): approx = jnp.dot(basis, q_new.T, precision=highest)]
    another operation x5 -> x0, other arithmetic: 6.68 us -> none  [the longest x3 3.6 us: on_device(): lower = jnp.linalg.cholesky(gram)]
  transfers between devices with their start and end apart: 1 -> 0, of which waited for: 1 -> 0; matrix products, arithmetic and copies ran while one was open for 0% -> 0% of each run, Pallas kernels for 0% -> 0%
where the time goes in v1:
time: 51.7 us; the launch traced here: 51.6 us
  Pallas kernels  50.2 us (97%)
  local copies, waits for them, and re-layouts  0.71 us (1%)
  between operations  0.65 us (1%)
    pallas_call x1, Pallas kernels, share(): pl.pallas_call(share_kernel, name='share', out_shape=(pltpu.VMEM((D, COLS...  46.9 us
    pallas_call x1, Pallas kernels, finish(): pl.pallas_call(body, name='finish', out_shape=(jax.ShapeDtypeStruct((own,...  3.29 us

profile of v1, /device:TPU:1, one launch (start us, length us, event | category | flops | bytes accessed | tf_op | source)
XLA Modules:
  0.0 51.6 jit_solution(11700785590486886895)
XLA Ops:
  0.6 0.0 copy-start
  0.6 0.7 %copy-done = f32[128,32]{0,1:T(8,128)S(1)} copy-done((f32[128,32]{0,1:T(8,128)S(1)}, f32[128,32]{0,1:T(8,128)}, u32[]{:S(2)}) %copy-start) | copy-done | bytes 16408
  1.3 46.9 %share.1 = (f32[8192,128]{1,0:T(8,128)S(1)}, bf16[8192,128]{1,0:T(8,128)(2,1)S(1)}, f32[32,32]{1,0:T(8,128)S(1)}, f32[32,128]{1,0:T(8,128)S(1)}) custom-call(f32[32,128]{1,0:T(8,128)S(1)} %bitcast.2, bf16[1,8192,128]{2,1,0:T(8,128)(2,1)} %g_hbm.1, f32[1,8192,128]{2,1,0:T(8,128)} %e_hbm.1), custom_call_target="tpu_custom_call" | custom-call | tf_op jit(solution)/shard_map/share/pallas_call | solution.py:276
  48.3 3.3 %finish.1 = (bf16[512,128]{1,0:T(8,128)(2,1)}, f32[1,8192,128]{2,1,0:T(8,128)}, f32[32,128]{1,0:T(8,128)}) custom-call(f32[8192,128]{1,0:T(8,128)S(1)} %get-tuple-element.10.refs_0_, bf16[8192,128]{1,0:T(8,128)(2,1)S(1)} %get-tuple-element.11.refs_1_, f32[32,32]{1,0:T(8,128)S(1)} %get-tuple-element.12.refs_2_, f32[32,128]{1,0:T(8,128)S(1)} %get-tuple-element.13.refs_3_), custom_call_target="tpu_custom_call" | custom-call | tf_op jit(solution)/shard_map/finish/pallas_call | solution.py:349
Async XLA Ops:
  0.6 0.7 %copy-start = (f32[128,32]{0,1:T(8,128)S(1)}, f32[128,32]{0,1:T(8,128)}, u32[]{:S(2)}) copy-start(f32[128,32]{0,1:T(8,128)} %param.5) | copy-start | bytes 49156

commit v2 on v0

v2 whole, which is shorter than its diff:
```python
import jax
import jax.numpy as jnp
from jax import lax
from jax.experimental import pallas as pl
from jax.experimental.pallas import tpu as pltpu
from jax.sharding import PartitionSpec as P

MESH = pl.DeviceIdType.MESH
F32, BF16 = jnp.float32, jnp.bfloat16
D, COLS, RANK = 8192, 128, 32
X, Y, Z = 4, 4, 8
GROUPS = COLS // RANK
ROWS = D // GROUPS
HALF = ROWS // 2
CHUNK = 512
NC = HALF // CHUNK
UNIT = 512
STREAMS = (("xy", 48), ("z", 32))
PLANE = sorted(
    [(i, j) for j in range(Y) for i in range(X) if (i, j) != (0, 0)],
    key=lambda o: -(min(o[0], X - o[0]) + min(o[1], Y - o[1])),
)
LINE = (4, 3, 5, 2, 6, 1, 7)
MEMBERS = {"xy": X * Y, "z": Z}
OTHER = {"xy": "z", "z": "xy"}
NN = (((1,), (0,)), ((), ()))
NT = (((1,), (1,)), ((), ()))
TN = (((0,), (0,)), ((), ()))


def dot(a, b, dims=NN, precision=None):
    return lax.dot_general(a, b, dims, precision=precision, preferred_element_type=F32)


def pair(value):
    hi = value.astype(BF16)
    return hi, (value - hi.astype(F32)).astype(BF16)


def quarters(value, rows, columns):
    return (
        value[:rows, :columns]
        + value[:rows, columns:]
        + value[rows:, :columns]
        + value[rows:, columns:]
    )


def inverse_factor(gram):
    n = gram.shape[0]
    row = lax.broadcasted_iota(jnp.int32, (n, n), 0)
    col = lax.broadcasted_iota(jnp.int32, (n, n), 1)
    left, right = gram, jnp.where(row == col, 1.0, 0.0).astype(F32)
    for k in range(n):
        scale = left[:, k : k + 1] / left[k : k + 1, k : k + 1]
        scale = jnp.where(row[:, :1] > k, scale, 0.0)
        left, right = (
            left - scale * left[k : k + 1, :],
            right - scale * right[k : k + 1, :],
        )
    pivots = jnp.sum(jnp.where(row == col, left, 0.0), axis=1, keepdims=True)
    return right / jnp.sqrt(pivots)


def share_kernel(
    q_hbm, g_hbm, e_hbm, merged, p_pair, linv_ref, ginv_ref, terms_ref,
    q_in, g_in, e_in, part, sib, summed, p_all, m_sib, s_pair, from_zt, t_mine, t_sib,
    g_mine, g_sib, ld_q, ld_g, ld_e, sib_s, sib_r, m_s, m_r, fw_s, fw_r, tz_s, tz_r, tc_s, tc_r, g_s, g_r, *per_stream,
):
    dp, me = lax.axis_index("dp"), lax.axis_index("tensor")
    x, y = lax.rem(me, X), lax.div(me, X)
    z, core = lax.div(dp, 2), lax.rem(dp, 2)
    other = 1 - core
    sibling = (z * 2 + other, me)
    hisrow, myrow = other * HALF, core * HALF
    place = {"xy": me, "z": z}
    offsets = {"xy": PLANE, "z": LINE}

    def member(axes, offset, back=False):
        if axes == "z":
            return lax.rem(z + (Z - offset if back else offset), Z)
        dx, dy = (X - offset[0], Y - offset[1]) if back else offset
        return lax.rem(y + dy, Y) * X + lax.rem(x + dx, X)

    def device(axes, index):
        return (dp, index) if axes == "xy" else (index * 2 + core, me)

    def remote(src, dst, send, recv, to):
        return pltpu.make_async_remote_copy(
            src_ref=src, dst_ref=dst, send_sem=send, recv_sem=recv, device_id=to, device_id_type=MESH
        )

    def rows_of(start, size):
        return pl.ds(pl.multiple_of(start, 8), size)

    load_q = pltpu.make_async_copy(q_hbm, q_in, ld_q)
    load_q.start()
    loads = []
    for i in range(2 * NC):
        rows = rows_of((hisrow if i < NC else myrow) + (i % NC) * CHUNK, CHUNK)
        both = (
            pltpu.make_async_copy(g_hbm.at[:, rows], g_in.at[:, rows], ld_g.at[i]),
            pltpu.make_async_copy(e_hbm.at[:, rows], e_in.at[:, rows], ld_e.at[i]),
        )
        for c in both:
            c.start()
        loads.append(both)

    barrier = pltpu.get_barrier_semaphore()
    pl.semaphore_signal(barrier, inc=1, device_id=sibling, device_id_type=MESH)
    for axes in ("xy", "z"):
        for o in offsets[axes]:
            pl.semaphore_signal(barrier, inc=1, device_id=device(axes, member(axes, o)), device_id_type=MESH)

    load_q.wait()
    qh, ql = pair(q_in[...])
    q_left = jnp.concatenate(
        [jnp.concatenate([qh, qh], axis=1), jnp.concatenate([ql, ql], axis=1)], axis=0
    )

    def partial(i):
        for c in loads[i]:
            c.wait()
        first = (hisrow if i < NC else myrow) + (i % NC) * CHUNK
        rows = rows_of(first, CHUNK)
        for g in range(GROUPS):
            total = g_in[g, rows].astype(F32) + e_in[g, rows]
            merged[g, rows] = total
            out = dot(q_left, jnp.concatenate(pair(total), axis=1), NT)
            out = out[:RANK] + out[RANK:]
            for b in range(CHUNK // COLS):
                part[rows_of(first + b * COLS + g * RANK, RANK)] = out[:, b * COLS : (b + 1) * COLS]

    def to_sibling(i):
        return remote(part.at[rows_of(hisrow + i * CHUNK, CHUNK)], sib.at[pl.ds(i * CHUNK, CHUNK)],
                      sib_s.at[i], sib_r.at[i], sibling)

    def m_to_sibling(g):
        return remote(merged.at[g, rows_of(hisrow, HALF)], m_sib.at[g], m_s, m_r, sibling)

    for i in range(NC):
        partial(i)
        if i == 0:
            pl.semaphore_wait(barrier, X * Y + Z - 1)
        to_sibling(i).start()
    for g in range(GROUPS):
        m_to_sibling(g).start()
    for i in range(NC):
        partial(NC + i)
    for i in range(NC):
        to_sibling(i).wait_recv()
        at = pl.ds(i * CHUNK, CHUNK)
        summed[at] = part[rows_of(myrow + i * CHUNK, CHUNK)] + sib[at]

    streams = []
    base = 0
    for n, (axes, size) in enumerate(STREAMS):
        streams.append((axes, size, base, *per_stream[8 * n : 8 * n + 8]))
        base += MEMBERS[axes] * size
    assert base == HALF

    def scatter(stream, j):
        axes, size, base, inbox, _, s1, r1, *_ = stream
        to = member(axes, offsets[axes][j])
        return remote(summed.at[rows_of(base + to * size, size)], inbox.at[j], s1, r1, device(axes, to))

    def exchange(stream, j):
        axes, size, base, _, box, _, _, s2, r2, _, _ = stream
        axes = OTHER[axes]
        mine = box.at[place[axes]]
        return remote(mine, mine, s2, r2, device(axes, member(axes, offsets[axes][j])))

    def gather(stream, j):
        axes, size, base, *_, s3, r3 = stream
        piece = p_all.at[rows_of(myrow + base + place[axes] * size, size)]
        return remote(piece, piece, s3, r3, device(axes, member(axes, offsets[axes][j])))

    def whole(stream, step):
        axes, size, base, inbox, box, s1, r1, s2, r2, s3, r3 = stream
        n = count(stream, step)
        what = inbox if step == 1 else box.at[pl.ds(0, n)] if step == 2 else p_all.at[pl.ds(0, n * size)]
        send, recv = ((s1, r1), (s2, r2), (s3, r3))[step - 1]
        return remote(what, what, send, recv, sibling)

    def count(stream, step):
        return MEMBERS[OTHER[stream[0]] if step == 2 else stream[0]] - 1

    for j in range(X * Y - 1):
        for stream in streams:
            if j < count(stream, 1):
                scatter(stream, j).start()

    for stream in streams:
        axes, size, base, inbox, box, *_ = stream
        total = summed[rows_of(base + place[axes] * size, size)]
        whole(stream, 1).wait_recv()
        for j in range(count(stream, 1)):
            total = total + inbox[j]
        box[place[OTHER[axes]]] = total
        for j in range(count(stream, 2)):
            exchange(stream, j).start()

    all_m = remote(m_sib, m_sib, m_s, m_r, sibling)
    all_m.wait_recv()

    def chip_pairs(i, _):
        at = pl.ds(pl.multiple_of(i * UNIT, UNIT), UNIT)
        for g in range(GROUPS):
            hi, lo = pair(merged[g, rows_of(myrow + i * UNIT, UNIT)] + m_sib[g, at])
            s_pair[g, at] = jnp.concatenate([hi, lo], axis=1)
        return 0

    lax.fori_loop(0, HALF // UNIT, chip_pairs, 0)

    for stream in streams:
        axes, size, base, inbox, box, *_ = stream
        whole(stream, 2).wait_recv()
        total = box[0]
        for j in range(1, MEMBERS[OTHER[axes]]):
            total = total + box[j]
        p_all[rows_of(myrow + base + place[axes] * size, size)] = total
        for j in range(count(stream, 3)):
            gather(stream, j).start()

    for stream in streams:
        whole(stream, 3).wait_recv()

    def forward(base):
        half = p_all.at[rows_of(base, HALF)]
        return remote(half, half, fw_s, fw_r, sibling)

    forward(myrow).start()

    def turned(base):
        blocks = [p_all[rows_of(base + b * COLS, COLS)] for b in range(HALF // COLS)]
        return blocks, pair(jnp.concatenate(blocks, axis=1))

    def store_rows(base, blocks):
        for b, block in enumerate(blocks):
            p_pair[rows_of(base + b * COLS, COLS)] = jnp.concatenate(pair(block.T), axis=1)

    blocks, halves = turned(myrow)
    left = [
        jnp.concatenate([v[g * RANK : (g + 1) * RANK] for g in range(GROUPS)], axis=1) for v in halves
    ]
    acc = dot(jnp.concatenate(left, axis=0), s_pair[...].reshape(GROUPS * HALF, 2 * COLS))
    from_zt[z] = quarters(acc, RANK, COLS)

    def terms_along(j):
        to = member("z", LINE[j])
        return remote(from_zt.at[z], from_zt.at[z], tz_s, tz_r, device("z", to))

    others = from_zt.at[pl.ds(0, Z - 1)]
    all_terms = remote(others, others, tz_s, tz_r, sibling)

    for j in range(Z - 1):
        terms_along(j).start()

    both = jnp.concatenate(halves, axis=0)
    gram = quarters(dot(both, both, NT), COLS, COLS)
    small = gram[:RANK, :RANK]
    for g in range(1, GROUPS):
        small = small + gram[g * RANK : (g + 1) * RANK, g * RANK : (g + 1) * RANK]
    g_mine[...] = small
    swap = remote(g_mine, g_sib, g_s, g_r, sibling)
    swap.start()
    store_rows(myrow, blocks)
    swap.wait()
    small = g_mine[...] + g_sib[...]
    linv = inverse_factor(small)
    linv_ref[...] = linv
    ginv_ref[...] = dot(linv, linv, TN, lax.Precision.HIGHEST)
    forward(hisrow).wait_recv()
    store_rows(hisrow, turned(hisrow)[0])

    for i in range(NC):
        to_sibling(i).wait_send()
    all_m.wait_send()
    for stream in streams:
        for step in (1, 2, 3):
            whole(stream, step).wait_send()
    forward(myrow).wait_send()

    all_terms.wait_recv()
    total = from_zt[0]
    for k in range(1, Z):
        total = total + from_zt[k]
    t_mine[...] = total
    last = remote(t_mine, t_sib, tc_s, tc_r, sibling)
    last.start()
    all_terms.wait_send()
    last.wait()
    terms_ref[...] = t_mine[...] + t_sib[...]


def share(q_t, grads, error):
    sems = pltpu.SemaphoreType.DMA
    hbm = pl.BlockSpec(memory_space=pltpu.HBM)
    args = (q_t, grads.reshape(GROUPS, ROWS, COLS), error.reshape(GROUPS, ROWS, COLS))
    per_stream = []
    for axes, size in STREAMS:
        first, second = MEMBERS[axes], MEMBERS[OTHER[axes]]
        per_stream += [
            pltpu.VMEM((first - 1, size, COLS), F32),
            pltpu.VMEM((second, size, COLS), F32),
            sems, sems, sems, sems, sems, sems,
        ]
    return pl.pallas_call(
        share_kernel,
        name="share",
        out_shape=(
            pltpu.VMEM((GROUPS, ROWS, COLS), F32),
            pltpu.VMEM((ROWS, 2 * COLS), BF16),
            pltpu.VMEM((RANK, RANK), F32),
            pltpu.VMEM((RANK, RANK), F32),
            pltpu.VMEM((RANK, COLS), F32),
        ),
        in_specs=[hbm] * 3,
        out_specs=[pl.BlockSpec(memory_space=pltpu.VMEM)] * 5,
        scratch_shapes=[
            pltpu.VMEM((RANK, COLS), F32),
            pltpu.VMEM((GROUPS, ROWS, COLS), BF16),
            pltpu.VMEM((GROUPS, ROWS, COLS), F32),
            pltpu.VMEM((ROWS, COLS), F32),
            pltpu.VMEM((HALF, COLS), F32),
            pltpu.VMEM((HALF, COLS), F32),
            pltpu.VMEM((ROWS, COLS), F32),
            pltpu.VMEM((GROUPS, HALF, COLS), F32),
            pltpu.VMEM((GROUPS, HALF, 2 * COLS), BF16),
            pltpu.VMEM((Z, RANK, COLS), F32),
            pltpu.VMEM((RANK, COLS), F32),
            pltpu.VMEM((RANK, COLS), F32),
            pltpu.VMEM((RANK, RANK), F32),
            pltpu.VMEM((RANK, RANK), F32),
            sems, sems((2 * NC,)), sems((2 * NC,)),
            sems((NC,)), sems((NC,)), sems, sems, sems, sems,
            sems, sems, sems, sems, sems, sems,
            *per_stream,
        ],
        compiler_params=pltpu.CompilerParams(
            collective_id=0, has_side_effects=True, vmem_limit_bytes=32 * 1024 * 1024
        ),
    )(*(pltpu.with_memory_space_constraint(a, pltpu.HBM) for a in args))


def finish_kernel(
    replicas, merged, p_pair, linv_ref, ginv_ref, terms_ref, synced, error_out, q_ref, right, out, rows_out, sem, sem_rows
):
    dp = lax.axis_index("dp")
    highest = lax.Precision.HIGHEST
    right[...] = jnp.zeros_like(right)
    terms = terms_ref[...] / replicas
    hi, lo = pair(dot(ginv_ref[...], terms, precision=highest))
    both = jnp.concatenate([hi, lo], axis=1)
    for g in range(GROUPS):
        right[g, pl.ds(g * RANK, RANK)] = both
        right[g, pl.ds(COLS + g * RANK, RANK)] = both

    def approx(g, rows):
        wide = dot(p_pair[rows], right[g])
        return wide[:, :COLS] + wide[:, COLS:]

    copies = []
    units = [(g, i * UNIT) for i in range(ROWS // UNIT) for g in range(GROUPS)]
    for n, (g, first) in enumerate(units):
        rows = pl.ds(first, UNIT)
        out[g, rows] = merged[g, rows] - approx(g, rows)
        copies.append(pltpu.make_async_copy(out.at[g, rows], error_out.at[g, rows], sem.at[n]))
        copies[-1].start()
        if n == len(units) // 2:
            own = D // replicas
            per = ROWS // own
            rows = pl.ds(pl.multiple_of(lax.rem(dp, per) * own, own), own)
            rows_out[...] = approx(lax.div(dp, per), rows).astype(BF16)
            copies.append(pltpu.make_async_copy(rows_out, synced, sem_rows))
            copies[-1].start()
    q_ref[...] = dot(linv_ref[...], terms, precision=highest)
    for c in copies:
        c.wait()


def finish(replicas, *operands):
    def body(*refs):
        finish_kernel(replicas, *refs)

    sems = pltpu.SemaphoreType.DMA
    own = D // replicas
    vmem, hbm = pl.BlockSpec(memory_space=pltpu.VMEM), pl.BlockSpec(memory_space=pl.ANY)
    return pl.pallas_call(
        body,
        name="finish",
        out_shape=(
            jax.ShapeDtypeStruct((own, COLS), BF16),
            jax.ShapeDtypeStruct((GROUPS, ROWS, COLS), F32),
            jax.ShapeDtypeStruct((RANK, COLS), F32),
        ),
        in_specs=[vmem] * 5,
        out_specs=[hbm, hbm, vmem],
        scratch_shapes=[
            pltpu.VMEM((GROUPS, 2 * COLS, 2 * COLS), BF16),
            pltpu.VMEM((GROUPS, ROWS, COLS), F32),
            pltpu.VMEM((own, COLS), BF16),
            sems((D // UNIT,)),
            sems,
        ],
        compiler_params=pltpu.CompilerParams(vmem_limit_bytes=16 * 1024 * 1024),
    )(*(pltpu.with_memory_space_constraint(a, pltpu.VMEM) for a in operands))


def solution(mesh):
    replicas = mesh.shape["dp"]

    def on_device(grads, error, q_prev):
        synced, error_out, q_t = finish(replicas, *share(q_prev.T, grads, error))
        return synced, error_out.reshape(1, D, COLS), q_t.T

    placed = (P("dp", None, "tensor"), P("dp", None, "tensor"), P("tensor", None))
    return jax.shard_map(
        on_device,
        mesh=mesh,
        in_specs=placed,
        out_specs=(P("dp", "tensor"), P("dp", None, "tensor"), P("tensor", None)),
        check_vma=False,
    )
```

time: 356 us -> 43.5 us (0.12)
  waiting for transfers between devices: 258 us -> 0 us
  blocking collectives: 45.6 us -> 0 us
  Pallas kernels: 0 us -> 42.8 us
  matrix products: 27.6 us -> 0 us
  between operations: 14.1 us -> 0.64 us
  other arithmetic: 6.69 us -> 0 us
    psum x1 -> x0, waiting for transfers between devices: 258 us -> none  [on_device(): p_whole = lax.psum(partial_p, ('dp', 'tensor'))]
    psum x1 -> x0, blocking collectives: 45.6 us -> none  [on_device(): q_new = lax.psum(q_terms, 'dp') / replicas]
    pallas_call x0 -> x2, Pallas kernels: none -> 42.8 us  [the longest x1 39.6 us: share(): pl.pallas_call(share_kernel, name='share', out_shape=(pltpu.VMEM((GROUPS,...]
    dot_general x4 -> x0, matrix products: 25.3 us -> none  [the longest x1 9.81 us: on_device(): approx = jnp.dot(basis, q_new.T, precision=highest)]
    another operation x5 -> x0, other arithmetic: 6.68 us -> none  [the longest x3 3.6 us: on_device(): lower = jnp.linalg.cholesky(gram)]
  transfers between devices with their start and end apart: 1 -> 0, of which waited for: 1 -> 0; matrix products, arithmetic and copies ran while one was open for 0% -> 0% of each run, Pallas kernels for 0% -> 0%
where the time goes in v2:
time: 43.5 us; the launch traced here: 43.4 us
  Pallas kernels  42.8 us (98%)
  between operations  0.64 us (1%)
    pallas_call x1, Pallas kernels, share(): pl.pallas_call(share_kernel, name='share', out_shape=(pltpu.VMEM((GROUPS,...  39.6 us
    pallas_call x1, Pallas kernels, finish(): pl.pallas_call(body, name='finish', out_shape=(jax.ShapeDtypeStruct((own,...  3.22 us

profile of v2, /device:TPU:1, one launch (start us, length us, event | category | flops | bytes accessed | tf_op | source)
XLA Modules:
  0.0 43.4 jit_solution(6246635802197061711)
XLA Ops:
  0.6 39.6 %share.1 = (f32[4,2048,128]{2,1,0:T(8,128)S(1)}, bf16[2048,256]{1,0:T(8,128)(2,1)S(1)}, f32[32,32]{1,0:T(8,128)S(1)}, f32[32,32]{1,0:T(8,128)S(1)}, f32[32,128]{1,0:T(8,128)S(1)}) custom-call(f32[32,128]{1,0:T(8,128)} %bitcast.7, bf16[4,2048,128]{2,1,0:T(8,128)(2,1)} %bitcast.6, f32[4,2048,128]{2,1,0:T(8,128)} %bitcast.5), custom_call_target="tpu_custom_call" | custom-call | tf_op jit(solution)/shard_map/share/pallas_call | solution.py:308
  40.2 3.2 %finish.1 = (bf16[512,128]{1,0:T(8,128)(2,1)}, f32[4,2048,128]{2,1,0:T(8,128)}, f32[32,128]{1,0:T(8,128)}) custom-call(f32[4,2048,128]{2,1,0:T(8,128)S(1)} %get-tuple-element.11.refs_0_, bf16[2048,256]{1,0:T(8,128)(2,1)S(1)} %get-tuple-element.12.refs_1_, f32[32,32]{1,0:T(8,128)S(1)} %get-tuple-element.13.refs_2_, f32[32,32]{1,0:T(8,128)S(1)} %get-tuple-element.14.refs_3_, ...), custom_call_target="tpu_custom_call" | custom-call | tf_op jit(solution)/shard_map/finish/pallas_call | solution.py:389

commit v3 on v2

--- a/solution.py
+++ b/solution.py
@@ -15,12 +15,12 @@
 CHUNK = 512
 NC = HALF // CHUNK
 UNIT = 512
-STREAMS = (("xy", 48), ("z", 32))
+STREAMS = (("z", 32), ("xy", 24), ("xy", 24))
 PLANE = sorted(
-    [(i, j) for j in range(Y) for i in range(X) if (i, j) != (0, 0)],
+    [(i, j) for j in range(Y) for i in range(X)],
     key=lambda o: -(min(o[0], X - o[0]) + min(o[1], Y - o[1])),
 )
-LINE = (4, 3, 5, 2, 6, 1, 7)
+LINE = (4, 3, 5, 2, 6, 1, 7, 0)
 MEMBERS = {"xy": X * Y, "z": Z}
 OTHER = {"xy": "z", "z": "xy"}
 NN = (((1,), (0,)), ((), ()))
@@ -64,8 +64,8 @@
 
 def share_kernel(
     q_hbm, g_hbm, e_hbm, merged, p_pair, linv_ref, ginv_ref, terms_ref,
-    q_in, g_in, e_in, part, sib, summed, p_all, m_sib, s_pair, from_zt, t_mine, t_sib,
-    g_mine, g_sib, ld_q, ld_g, ld_e, sib_s, sib_r, m_s, m_r, fw_s, fw_r, tz_s, tz_r, tc_s, tc_r, g_s, g_r, *per_stream,
+    q_in, g_in, e_in, part, sib, summed, p_all, m_sib, s_pair, from_zt, t_mine, t_sib, t_all,
+    g_mine, g_sib, ld_q, ld_g, ld_e, sib_s, sib_r, m_s, m_r, fw_s, fw_r, tz_s, tz_r, tu_s, tu_r, td_s, td_r, g_s, g_r, *per_stream,
 ):
     dp, me = lax.axis_index("dp"), lax.axis_index("tensor")
     x, y = lax.rem(me, X), lax.div(me, X)
@@ -83,7 +83,7 @@
         return lax.rem(y + dy, Y) * X + lax.rem(x + dx, X)
 
     def device(axes, index):
-        return (dp, index) if axes == "xy" else (index * 2 + core, me)
+        return (z * 2 + other, index) if axes == "xy" else (index * 2 + other, me)
 
     def remote(src, dst, send, recv, to):
         return pltpu.make_async_remote_copy(
@@ -107,10 +107,11 @@
         loads.append(both)
 
     barrier = pltpu.get_barrier_semaphore()
-    pl.semaphore_signal(barrier, inc=1, device_id=sibling, device_id_type=MESH)
-    for axes in ("xy", "z"):
-        for o in offsets[axes]:
-            pl.semaphore_signal(barrier, inc=1, device_id=device(axes, member(axes, o)), device_id_type=MESH)
+    greeted = [device("xy", member("xy", o)) for o in PLANE]
+    for o in LINE[:-1]:
+        greeted += [device("z", member("z", o)), (member("z", o) * 2 + core, me)]
+    for to in greeted:
+        pl.semaphore_signal(barrier, inc=1, device_id=to, device_id_type=MESH)
 
     load_q.wait()
     qh, ql = pair(q_in[...])
@@ -136,17 +137,17 @@
                       sib_s.at[i], sib_r.at[i], sibling)
 
     def m_to_sibling(g):
-        return remote(merged.at[g, rows_of(hisrow, HALF)], m_sib.at[g], m_s, m_r, sibling)
+        return remote(merged.at[g, rows_of(myrow, HALF)], m_sib.at[g], m_s, m_r, sibling)
 
     for i in range(NC):
         partial(i)
         if i == 0:
-            pl.semaphore_wait(barrier, X * Y + Z - 1)
+            pl.semaphore_wait(barrier, len(greeted))
         to_sibling(i).start()
+    for i in range(NC):
+        partial(NC + i)
     for g in range(GROUPS):
         m_to_sibling(g).start()
-    for i in range(NC):
-        partial(NC + i)
     for i in range(NC):
         to_sibling(i).wait_recv()
         at = pl.ds(i * CHUNK, CHUNK)
@@ -155,48 +156,46 @@
     streams = []
     base = 0
     for n, (axes, size) in enumerate(STREAMS):
-        streams.append((axes, size, base, *per_stream[8 * n : 8 * n + 8]))
+        streams.append((axes, size, base, *per_stream[10 * n : 10 * n + 10]))
         base += MEMBERS[axes] * size
     assert base == HALF
 
+    def count(stream, step):
+        return MEMBERS[OTHER[stream[0]] if step == 2 else stream[0]]
+
     def scatter(stream, j):
-        axes, size, base, inbox, _, s1, r1, *_ = stream
+        axes, size, base, inbox, _, _, _, s1, r1, *_ = stream
         to = member(axes, offsets[axes][j])
         return remote(summed.at[rows_of(base + to * size, size)], inbox.at[j], s1, r1, device(axes, to))
 
     def exchange(stream, j):
-        axes, size, base, _, box, _, _, s2, r2, _, _ = stream
+        axes, size, base, _, box, mid, _, _, _, s2, r2, _, _ = stream
         axes = OTHER[axes]
-        mine = box.at[place[axes]]
-        return remote(mine, mine, s2, r2, device(axes, member(axes, offsets[axes][j])))
+        return remote(mid, box.at[place[axes]], s2, r2, device(axes, member(axes, offsets[axes][j])))
 
     def gather(stream, j):
-        axes, size, base, *_, s3, r3 = stream
-        piece = p_all.at[rows_of(myrow + base + place[axes] * size, size)]
-        return remote(piece, piece, s3, r3, device(axes, member(axes, offsets[axes][j])))
+        axes, size, base, _, _, _, done, *_, s3, r3 = stream
+        target = p_all.at[rows_of(myrow + base + place[axes] * size, size)]
+        return remote(done, target, s3, r3, device(axes, member(axes, offsets[axes][j])))
 
     def whole(stream, step):
-        axes, size, base, inbox, box, s1, r1, s2, r2, s3, r3 = stream
-        n = count(stream, step)
-        what = inbox if step == 1 else box.at[pl.ds(0, n)] if step == 2 else p_all.at[pl.ds(0, n * size)]
+        axes, size, base, inbox, box, _, _, s1, r1, s2, r2, s3, r3 = stream
+        what = inbox if step == 1 else box if step == 2 else p_all.at[pl.ds(0, count(stream, 3) * size)]
         send, recv = ((s1, r1), (s2, r2), (s3, r3))[step - 1]
         return remote(what, what, send, recv, sibling)
 
-    def count(stream, step):
-        return MEMBERS[OTHER[stream[0]] if step == 2 else stream[0]] - 1
-
-    for j in range(X * Y - 1):
+    for j in range(X * Y):
         for stream in streams:
             if j < count(stream, 1):
                 scatter(stream, j).start()
 
     for stream in streams:
-        axes, size, base, inbox, box, *_ = stream
-        total = summed[rows_of(base + place[axes] * size, size)]
+        axes, size, base, inbox, box, mid, *_ = stream
         whole(stream, 1).wait_recv()
-        for j in range(count(stream, 1)):
+        total = inbox[0]
+        for j in range(1, count(stream, 1)):
             total = total + inbox[j]
-        box[place[OTHER[axes]]] = total
+        mid[...] = total
         for j in range(count(stream, 2)):
             exchange(stream, j).start()
 
@@ -206,19 +205,19 @@
     def chip_pairs(i, _):
         at = pl.ds(pl.multiple_of(i * UNIT, UNIT), UNIT)
         for g in range(GROUPS):
-            hi, lo = pair(merged[g, rows_of(myrow + i * UNIT, UNIT)] + m_sib[g, at])
+            hi, lo = pair(merged[g, rows_of(hisrow + i * UNIT, UNIT)] + m_sib[g, at])
             s_pair[g, at] = jnp.concatenate([hi, lo], axis=1)
         return 0
 
     lax.fori_loop(0, HALF // UNIT, chip_pairs, 0)
 
     for stream in streams:
-        axes, size, base, inbox, box, *_ = stream
+        axes, size, base, inbox, box, mid, done, *_ = stream
         whole(stream, 2).wait_recv()
         total = box[0]
-        for j in range(1, MEMBERS[OTHER[axes]]):
+        for j in range(1, count(stream, 2)):
             total = total + box[j]
-        p_all[rows_of(myrow + base + place[axes] * size, size)] = total
+        done[...] = total
         for j in range(count(stream, 3)):
             gather(stream, j).start()
 
@@ -229,8 +228,6 @@
         half = p_all.at[rows_of(base, HALF)]
         return remote(half, half, fw_s, fw_r, sibling)
 
-    forward(myrow).start()
-
     def turned(base):
         blocks = [p_all[rows_of(base + b * COLS, COLS)] for b in range(HALF // COLS)]
         return blocks, pair(jnp.concatenate(blocks, axis=1))
@@ -239,22 +236,18 @@
         for b, block in enumerate(blocks):
             p_pair[rows_of(base + b * COLS, COLS)] = jnp.concatenate(pair(block.T), axis=1)
 
-    blocks, halves = turned(myrow)
+    blocks, halves = turned(hisrow)
     left = [
         jnp.concatenate([v[g * RANK : (g + 1) * RANK] for g in range(GROUPS)], axis=1) for v in halves
     ]
     acc = dot(jnp.concatenate(left, axis=0), s_pair[...].reshape(GROUPS * HALF, 2 * COLS))
-    from_zt[z] = quarters(acc, RANK, COLS)
-
-    def terms_along(j):
-        to = member("z", LINE[j])
-        return remote(from_zt.at[z], from_zt.at[z], tz_s, tz_r, device("z", to))
-
-    others = from_zt.at[pl.ds(0, Z - 1)]
-    all_terms = remote(others, others, tz_s, tz_r, sibling)
-
-    for j in range(Z - 1):
-        terms_along(j).start()
+    t_mine[...] = quarters(acc, RANK, COLS)
+
+    up = remote(t_mine, t_sib, tu_s, tu_r, sibling)
+
+    @pl.when(core == 0)
+    def _():
+        up.start()
 
     both = jnp.concatenate(halves, axis=0)
     gram = quarters(dot(both, both, NT), COLS, COLS)
@@ -264,14 +257,25 @@
     g_mine[...] = small
     swap = remote(g_mine, g_sib, g_s, g_r, sibling)
     swap.start()
-    store_rows(myrow, blocks)
+    forward(hisrow).start()
+
+    others = from_zt.at[pl.ds(0, Z - 1)]
+    all_terms = remote(others, others, tz_s, tz_r, sibling)
+
+    @pl.when(core == 1)
+    def _():
+        up.wait_recv()
+        from_zt[z] = t_mine[...] + t_sib[...]
+        for o in LINE[:-1]:
+            remote(from_zt.at[z], from_zt.at[z], tz_s, tz_r, (member("z", o) * 2 + 1, me)).start()
+
+    store_rows(hisrow, blocks)
     swap.wait()
-    small = g_mine[...] + g_sib[...]
-    linv = inverse_factor(small)
+    linv = inverse_factor(g_mine[...] + g_sib[...])
     linv_ref[...] = linv
     ginv_ref[...] = dot(linv, linv, TN, lax.Precision.HIGHEST)
-    forward(hisrow).wait_recv()
-    store_rows(hisrow, turned(hisrow)[0])
+    forward(myrow).wait_recv()
+    store_rows(myrow, turned(myrow)[0])
 
     for i in range(NC):
         to_sibling(i).wait_send()
@@ -279,18 +283,27 @@
     for stream in streams:
         for step in (1, 2, 3):
             whole(stream, step).wait_send()
-    forward(myrow).wait_send()
-
-    all_terms.wait_recv()
-    total = from_zt[0]
-    for k in range(1, Z):
-        total = total + from_zt[k]
-    t_mine[...] = total
-    last = remote(t_mine, t_sib, tc_s, tc_r, sibling)
-    last.start()
-    all_terms.wait_send()
-    last.wait()
-    terms_ref[...] = t_mine[...] + t_sib[...]
+    forward(hisrow).wait_send()
+
+    down = remote(t_all, t_all, td_s, td_r, sibling)
+
+    @pl.when(core == 1)
+    def _():
+        all_terms.wait_recv()
+        total = from_zt[0]
+        for k in range(1, Z):
+            total = total + from_zt[k]
+        t_all[...] = total
+        down.start()
+        all_terms.wait_send()
+        down.wait_send()
+
+    @pl.when(core == 0)
+    def _():
+        up.wait_send()
+        down.wait_recv()
+
+    terms_ref[...] = t_all[...]
 
 
 def share(q_t, grads, error):
@@ -301,8 +314,10 @@
     for axes, size in STREAMS:
         first, second = MEMBERS[axes], MEMBERS[OTHER[axes]]
         per_stream += [
-            pltpu.VMEM((first - 1, size, COLS), F32),
+            pltpu.VMEM((first, size, COLS), F32),
             pltpu.VMEM((second, size, COLS), F32),
+            pltpu.VMEM((size, COLS), F32),
+            pltpu.VMEM((size, COLS), F32),
             sems, sems, sems, sems, sems, sems,
         ]
     return pl.pallas_call(
@@ -330,11 +345,12 @@
             pltpu.VMEM((Z, RANK, COLS), F32),
             pltpu.VMEM((RANK, COLS), F32),
             pltpu.VMEM((RANK, COLS), F32),
+            pltpu.VMEM((RANK, COLS), F32),
             pltpu.VMEM((RANK, RANK), F32),
             pltpu.VMEM((RANK, RANK), F32),
             sems, sems((2 * NC,)), sems((2 * NC,)),
             sems((NC,)), sems((NC,)), sems, sems, sems, sems,
-            sems, sems, sems, sems, sems, sems,
+            sems, sems, sems, sems, sems, sems, sems, sems,
             *per_stream,
         ],
         compiler_params=pltpu.CompilerParams(

time: 43.5 us -> 42.6 us (0.979)
  Pallas kernels: 42.8 us -> 41.9 us
    pallas_call x1, Pallas kernels: 39.6 us -> 38.7 us  [share(): pl.pallas_call(share_kernel, name='share', out_shape=(pltpu.VMEM((GROUPS,...]
where the time goes in v3:
time: 42.6 us
  Pallas kernels  41.9 us (98%)
  between operations  0.64 us (2%)
    pallas_call x1, Pallas kernels, share(): pl.pallas_call(share_kernel, name='share', out_shape=(pltpu.VMEM((GROUPS,...  38.7 us
    pallas_call x1, Pallas kernels, finish(): pl.pallas_call(body, name='finish', out_shape=(jax.ShapeDtypeStruct((own,...  3.22 us

profile of v3, /device:TPU:1, one launch (start us, length us, event | category | flops | bytes accessed | tf_op | source)
XLA Modules:
  0.0 42.6 jit_solution(8220567604787439502)
XLA Ops:
  0.6 38.7 %share.1 = (f32[4,2048,128]{2,1,0:T(8,128)S(1)}, bf16[2048,256]{1,0:T(8,128)(2,1)S(1)}, f32[32,32]{1,0:T(8,128)S(1)}, f32[32,32]{1,0:T(8,128)S(1)}, f32[32,128]{1,0:T(8,128)S(1)}) custom-call(f32[32,128]{1,0:T(8,128)} %bitcast.7, bf16[4,2048,128]{2,1,0:T(8,128)(2,1)} %bitcast.6, f32[4,2048,128]{2,1,0:T(8,128)} %bitcast.5), custom_call_target="tpu_custom_call" | custom-call | tf_op jit(solution)/shard_map/share/pallas_call | solution.py:323
  39.3 3.2 %finish.1 = (bf16[512,128]{1,0:T(8,128)(2,1)}, f32[4,2048,128]{2,1,0:T(8,128)}, f32[32,128]{1,0:T(8,128)}) custom-call(f32[4,2048,128]{2,1,0:T(8,128)S(1)} %get-tuple-element.11.refs_0_, bf16[2048,256]{1,0:T(8,128)(2,1)S(1)} %get-tuple-element.12.refs_1_, f32[32,32]{1,0:T(8,128)S(1)} %get-tuple-element.13.refs_2_, f32[32,32]{1,0:T(8,128)S(1)} %get-tuple-element.14.refs_3_, ...), custom_call_target="tpu_custom_call" | custom-call | tf_op jit(solution)/shard_map/finish/pallas_call | solution.py:405

commit v4 on v3

--- a/solution.py
+++ b/solution.py
@@ -12,7 +12,7 @@
 GROUPS = COLS // RANK
 ROWS = D // GROUPS
 HALF = ROWS // 2
-CHUNK = 512
+CHUNK = 1024
 NC = HALF // CHUNK
 UNIT = 512
 STREAMS = (("z", 32), ("xy", 24), ("xy", 24))
@@ -93,6 +93,13 @@
     def rows_of(start, size):
         return pl.ds(pl.multiple_of(start, 8), size)
 
+    barrier = pltpu.get_barrier_semaphore()
+    greeted = [device("xy", member("xy", o)) for o in PLANE]
+    for o in LINE[:-1]:
+        greeted += [device("z", member("z", o)), (member("z", o) * 2 + core, me)]
+    for to in greeted:
+        pl.semaphore_signal(barrier, inc=1, device_id=to, device_id_type=MESH)
+
     load_q = pltpu.make_async_copy(q_hbm, q_in, ld_q)
     load_q.start()
     loads = []
@@ -105,13 +112,6 @@
         for c in both:
             c.start()
         loads.append(both)
-
-    barrier = pltpu.get_barrier_semaphore()
-    greeted = [device("xy", member("xy", o)) for o in PLANE]
-    for o in LINE[:-1]:
-        greeted += [device("z", member("z", o)), (member("z", o) * 2 + core, me)]
-    for to in greeted:
-        pl.semaphore_signal(barrier, inc=1, device_id=to, device_id_type=MESH)
 
     load_q.wait()
     qh, ql = pair(q_in[...])

time: 42.6 us -> 42.6 us (level)
  no operation moved by 1% of the time
where the time goes in v4:
time: 42.6 us; the launch traced here: 42.5 us
  Pallas kernels  41.9 us (98%)
  between operations  0.64 us (2%)
    pallas_call x1, Pallas kernels, share(): pl.pallas_call(share_kernel, name='share', out_shape=(pltpu.VMEM((GROUPS,...  38.7 us
    pallas_call x1, Pallas kernels, finish(): pl.pallas_call(body, name='finish', out_shape=(jax.ShapeDtypeStruct((own,...  3.22 us

profile of v4, /device:TPU:1, one launch (start us, length us, event | category | flops | bytes accessed | tf_op | source)
XLA Modules:
  0.0 42.5 jit_solution(2310669832574520703)
XLA Ops:
  0.6 38.7 %share.1 = (f32[4,2048,128]{2,1,0:T(8,128)S(1)}, bf16[2048,256]{1,0:T(8,128)(2,1)S(1)}, f32[32,32]{1,0:T(8,128)S(1)}, f32[32,32]{1,0:T(8,128)S(1)}, f32[32,128]{1,0:T(8,128)S(1)}) custom-call(f32[32,128]{1,0:T(8,128)} %bitcast.7, bf16[4,2048,128]{2,1,0:T(8,128)(2,1)} %bitcast.6, f32[4,2048,128]{2,1,0:T(8,128)} %bitcast.5), custom_call_target="tpu_custom_call" | custom-call | tf_op jit(solution)/shard_map/share/pallas_call | solution.py:323
  39.3 3.2 %finish.1 = (bf16[512,128]{1,0:T(8,128)(2,1)}, f32[4,2048,128]{2,1,0:T(8,128)}, f32[32,128]{1,0:T(8,128)}) custom-call(f32[4,2048,128]{2,1,0:T(8,128)S(1)} %get-tuple-element.11.refs_0_, bf16[2048,256]{1,0:T(8,128)(2,1)S(1)} %get-tuple-element.12.refs_1_, f32[32,32]{1,0:T(8,128)S(1)} %get-tuple-element.13.refs_2_, f32[32,32]{1,0:T(8,128)S(1)} %get-tuple-element.14.refs_3_, ...), custom_call_target="tpu_custom_call" | custom-call | tf_op jit(solution)/shard_map/finish/pallas_call | solution.py:405
